TPU v7x, 32 devices: a whole 2x2x4 slice. The times are simulated.
32 devices in a mesh: groups: 2 (over y), blk: 4 (over z), sub: 4 (over x, core).
Axes of the slice: x: 2, y: 2, z: 4, core: 2. Of those that a mesh axis runs over, the one named last changes fastest.
Arguments:
- dense_coef: float32 [256, 128, 128], P(('groups', 'blk'), 'sub'), parts along dimension 0, may hold values from -6 to 6
- sparse_coef: float32 [8, 128, 128], P(('groups', 'blk'), 'sub'), parts along dimension 0, may hold values from -0.0234375 to 0.0234375
- pattern: int32 [8], P('groups'), parts along dimension 0, may hold values from 0 to 159, as said below
Outputs:
- product_coef: float32 [256, 128, 128], P(('groups', 'blk'), 'sub'), parts along dimension 0
There are 2 independent parts, one for each index of `groups`. A program takes and returns all parts, laid end to end along the dimension named above; each array names one. Nothing has to cross between parts.
Inputs may be any that keep to these rules, and one draw needn't show every extreme that they name: `pattern`: the 4 entries are distinct.
All inputs are finite; a program needn't handle non-finite values.
Results may differ from a plain program's by a relative error of at most 0.000076.
Values sent between devices are 32-bit elements; how exact they have to be, the bound alone decides.
A program may use at most 128 MiB of HBM per device.

v0:
```python
import math

import jax
import jax.numpy as jnp
from jax import lax
from jax.sharding import PartitionSpec as P

STEPS = 5


exact_setting = lax.Precision.HIGHEST


def shifted(block, axis, distance):
    devices = range(lax.axis_size(axis))
    route = [((i - distance) % len(devices), i) for i in devices]
    return lax.ppermute(block, axis, route)


def angle_table(row_total, col_total, period, row_start, col_start):
    row_ids = jnp.arange(row_total, dtype=jnp.int32)[:, None] + row_start
    col_ids = jnp.arange(col_total, dtype=jnp.int32)[None, :] + col_start
    phases = jnp.mod(row_ids * col_ids, period).astype(jnp.float32) * (2.0 * math.pi / period)
    return (jnp.cos(phases), jnp.sin(phases))


def forward(series_coefficients):
    col_local = series_coefficients.shape[1]
    row_total = series_coefficients.shape[2]
    padded = 2 * row_total
    col_total = col_local * lax.axis_size("sub")
    period = padded * col_total
    cosine_lookup, sine_lookup = angle_table(row_total, padded, padded, 0, 0)
    initial_real = jnp.einsum(
        "ufz,ze->ufe", series_coefficients, cosine_lookup, precision=exact_setting
    )
    initial_imaginary = -jnp.einsum(
        "ufz,ze->ufe", series_coefficients, sine_lookup, precision=exact_setting
    )
    twist_cos, twist_sin = angle_table(
        col_local, padded, period, lax.axis_index("sub") * col_local, 0
    )
    turned_real = initial_real * twist_cos + initial_imaginary * twist_sin
    turned_imag = initial_imaginary * twist_cos - initial_real * twist_sin
    stacked = jnp.stack([turned_real, turned_imag], axis=0)
    outer_cosine, outer_sine = angle_table(col_total, col_total, col_total, 0, 0)
    halves = lax.all_to_all(stacked, "sub", split_axis=3, concat_axis=2, tiled=True)
    partial_real = halves[0]
    partial_imaginary = halves[1]
    output_real = jnp.einsum(
        "rxs,xl->rsl", partial_real, outer_cosine, precision=exact_setting
    ) + jnp.einsum("rxs,xl->rsl", partial_imaginary, outer_sine, precision=exact_setting)
    output_imaginary = jnp.einsum(
        "rxs,xl->rsl", partial_imaginary, outer_cosine, precision=exact_setting
    ) - jnp.einsum("rxs,xl->rsl", partial_real, outer_sine, precision=exact_setting)
    return jnp.stack([output_real, output_imaginary], axis=0)


def flatten(halves):
    return (halves[0].reshape(halves[0].shape[0], -1), halves[1].reshape(halves[1].shape[0], -1))


def accumulate(totals, source, sparse, pattern, start):
    source_len = source[0].shape[0]
    targets = jnp.arange(totals[0].shape[0], dtype=jnp.int32)

    def one_entry(entry, running):
        wanted = start + targets - pattern[entry]
        valid = jnp.logical_and(wanted >= 0, wanted < source_len)[:, None]
        safe = jnp.clip(wanted, 0, source_len - 1)
        src_real = jnp.where(valid, jnp.take(source[0], safe, axis=0), 0.0)
        src_imag = jnp.where(valid, jnp.take(source[1], safe, axis=0), 0.0)
        sp_real = sparse[0][entry][None, :]
        sp_imag = sparse[1][entry][None, :]
        return (
            running[0] + src_real * sp_real - src_imag * sp_imag,
            running[1] + src_real * sp_imag + src_imag * sp_real,
        )

    return lax.fori_loop(0, pattern.shape[0], one_entry, totals)


def inverse(totals, local_rows, col_total):
    block_count = totals[0].shape[0]
    spectrum_real = totals[0].reshape(block_count, local_rows, col_total)
    spectrum_imaginary = totals[1].reshape(block_count, local_rows, col_total)
    padded = local_rows * lax.axis_size("sub")
    period = padded * col_total
    outer_cosine, outer_sine = angle_table(col_total, col_total, col_total, 0, 0)
    combined_real = jnp.einsum(
        "ahz,zr->arh", spectrum_real, outer_cosine, precision=exact_setting
    ) - jnp.einsum("ahz,zr->arh", spectrum_imaginary, outer_sine, precision=exact_setting)
    combined_imaginary = jnp.einsum(
        "ahz,zr->arh", spectrum_real, outer_sine, precision=exact_setting
    ) + jnp.einsum("ahz,zr->arh", spectrum_imaginary, outer_cosine, precision=exact_setting)
    twist_cos, twist_sin = angle_table(
        col_total, local_rows, period, 0, lax.axis_index("sub") * local_rows
    )
    turned_real = combined_real * twist_cos - combined_imaginary * twist_sin
    turned_imag = combined_real * twist_sin + combined_imaginary * twist_cos
    inverse_step_real, inverse_step_imaginary = (
        lax.all_to_all(turned_real, "sub", split_axis=1, concat_axis=2, tiled=True),
        lax.all_to_all(turned_imag, "sub", split_axis=1, concat_axis=2, tiled=True),
    )
    closing_cosine, closing_sine = angle_table(padded, padded, padded, 0, 0)
    value_entries = jnp.einsum(
        "xmj,jo->xmo", inverse_step_real, closing_cosine, precision=exact_setting
    ) - jnp.einsum("xmj,jo->xmo", inverse_step_imaginary, closing_sine, precision=exact_setting)
    return value_entries / period


def local(dense_coef, sparse_coef, pattern):
    block_count = dense_coef.shape[0]
    row_total = dense_coef.shape[2]
    spectra = forward(dense_coef)
    spec_shape = spectra[0].shape
    sparse = flatten(lax.all_gather(forward(sparse_coef), "blk", axis=1, tiled=True))
    empty_sum = jnp.zeros((block_count, spec_shape[1] * spec_shape[2]), jnp.float32)
    totals = (empty_sum, empty_sum)
    current = spectra
    for turn_index in range(STEPS + 1):
        if turn_index > 0:
            current = shifted(current, "blk", 1)
        totals = accumulate(totals, flatten(current), sparse, pattern, turn_index * block_count)
    value_entries = inverse(totals, spec_shape[1], spec_shape[2])
    lower_half = value_entries[:, :, :row_total]
    upper_half = value_entries[:, :, row_total:]
    carried_in = shifted(upper_half[-1:], "blk", 1)
    return lower_half + jnp.concatenate([carried_in, upper_half[:-1]], axis=0)


def solution(mesh):
    return jax.shard_map(
        local,
        mesh=mesh,
        in_specs=(
            P(("groups", "blk"), "sub", None),
            P(("groups", "blk"), "sub", None),
            P("groups"),
        ),
        out_specs=P(("groups", "blk"), "sub", None),
        check_vma=False,
    )
```

profile of v0, /device:TPU:0, one launch (start us, length us, event | category | flops | bytes accessed | tf_op | source)
XLA Modules:
  0.0 462.5 jit_solution(10227931367806987062)
XLA Ops:
  14.4 7.6 %copy.18 = f32[2,32,32,256]{2,1,0,3:T(8,128)} copy(f32[2,32,32,256]{3,2,1,0:T(8,128)S(1)} %pad_maximum_fusion) | data formatting | bytes 4194304 | tf_op jit(solution)/shard_map/stack | solution.py:45
  22.0 7.1 %reshape.364 = f32[4,1,131072]{2,1,0:T(1,128)} reshape(f32[256,2,32,32]{3,2,1,0:T(8,128)} %bitcast.225) | data formatting | bytes 4194304
  29.1 4.5 all-to-all-start
  36.8 15.2 %all_gather.3 = f32[2,4,64,128]{3,2,1,0:T(8,128)S(1)} all-gather(f32[2,1,64,128]{3,2,1,0:T(8,128)S(1)} %pad_maximum_fusion.3), channel_id=1, replica_groups=mesh['groups'=2,'blk'=4,'sub'=4] {'blk'}, dimensions={1}, use_global_device_ids=true | all-gather | bytes 327680 | tf_op jit(solution)/shard_map/all_gather | solution.py:117
  52.3 7.1 %all-to-all-done = f32[4,1,131072]{2,1,0:T(1,128)} async-done(((f32[4,1,131072]{2,1,0:T(1,128)}), f32[4,1,131072]{2,1,0:T(1,128)}, u32[]{:S(2)}, u32[]{:S(2)}) %all-to-all-start) | async-done | bytes 2097184 | tf_op jit(solution)/shard_map/all_to_all | solution.py:47
  59.4 7.7 %reduce = f32[4,131072]{1,0:T(4,128)S(1)} reduce(f32[4,1,131072]{2,1,0:T(1,128)} %all-to-all-done, f32[]{:T(128)} %broadcast.711), dimensions={1}, to_apply=%all_to_all.48.reduce_sub_computation | reduce | bytes 4194308 | tf_op jit(solution)/shard_map/all_to_all | solution.py:47
  67.1 6.2 %reshape.365 = f32[256,2,32,32]{3,2,1,0:T(8,128)} reshape(f32[4,131072]{1,0:T(4,128)S(1)} %reduce) | data formatting | bytes 4194304
  73.3 8.0 %copy.19 = f32[2,32,32,4,64]{4,2,3,1,0:T(8,128)} copy(f32[2,32,32,4,64]{2,1,0,4,3:T(8,128)} %bitcast.226) | data formatting | bytes 4194304 | tf_op jit(solution)/shard_map/all_to_all | solution.py:47
  103.1 36.4 %while.101 = (s32[]{:T(128)}, f32[32,8192]{1,0:T(8,128)S(1)}, f32[32,8192]{1,0:T(8,128)}, s32[4]{0:T(128)S(1)}, f32[32,8192]{1,0:T(8,128)S(1)}, /*index=5*/f32[4...) while((s32[]{:T(128)}, f32[32,8192]{1,0:T(8,128)S(1)}, ...), condition=%wide.region_1.3_spmd.clone, body=%wide.region_0.2_spmd.clone.sunk | while | flops 3671555 | bytes 10687239 | solution.py:80
  139.5 10.2 %collective-permute-done = f32[2,32,64,128]{3,2,1,0:T(8,128)} collective-permute-done((f32[2,32,64,128]{3,2,1,0:T(8,128)}, f32[2,32,64,128]{3,2,1,0:T(8,128)}, u32[]{:S(2)}, u32[]{:S(2)}) %collective-permute-start) | collective-permute-done | bytes 2097184 | tf_op jit(solution)/shard_map/ppermute | solution.py:17
  152.6 38.5 %while.96 = (s32[]{:T(128)}, f32[32,8192]{1,0:T(8,128)S(1)}, f32[32,8192]{1,0:T(8,128)}, s32[4]{0:T(128)S(1)}, f32[32,8192]{1,0:T(8,128)S(1)}, /*index=5*/f32[4,...) while((s32[]{:T(128)}, f32[32,8192]{1,0:T(8,128)S(1)}, ...), condition=%wide.region_3.5_spmd.clone, body=%wide.region_2.4_spmd.clone.sunk | while | flops 3147330 | bytes 10687221 | solution.py:80
  191.1 10.2 %collective-permute-done.1 = f32[2,32,64,128]{3,2,1,0:T(8,128)} collective-permute-done((f32[2,32,64,128]{3,2,1,0:T(8,128)}, f32[2,32,64,128]{3,2,1,0:T(8,128)}, u32[]{:S(2)}, u32[]{:S(2)}) %collective-permute-start.1) | collective-permute-done | bytes 2097184 | tf_op jit(solution)/shard_map/ppermute | solution.py:17
  204.2 38.9 %while.97 = (s32[]{:T(128)}, f32[32,8192]{1,0:T(8,128)S(1)}, f32[32,8192]{1,0:T(8,128)}, s32[4]{0:T(128)S(1)}, f32[32,8192]{1,0:T(8,128)S(1)}, /*index=5*/f32[4,...) while((s32[]{:T(128)}, f32[32,8192]{1,0:T(8,128)S(1)}, ...), condition=%wide.region_5.7_spmd.clone, body=%wide.region_4.6_spmd.clone.sunk | while | flops 3147330 | bytes 10687221 | solution.py:80
  243.2 8.8 %collective-permute-done.2 = f32[2,32,64,128]{3,2,1,0:T(8,128)} collective-permute-done((f32[2,32,64,128]{3,2,1,0:T(8,128)}, f32[2,32,64,128]{3,2,1,0:T(8,128)}, u32[]{:S(2)}, u32[]{:S(2)}) %collective-permute-start.2) | collective-permute-done | bytes 2097184 | tf_op jit(solution)/shard_map/ppermute | solution.py:17
  255.0 38.5 %while.98 = (s32[]{:T(128)}, f32[32,8192]{1,0:T(8,128)S(1)}, f32[32,8192]{1,0:T(8,128)}, s32[4]{0:T(128)S(1)}, f32[32,8192]{1,0:T(8,128)S(1)}, /*index=5*/f32[4,...) while((s32[]{:T(128)}, f32[32,8192]{1,0:T(8,128)S(1)}, ...), condition=%wide.region_7.9_spmd.clone, body=%wide.region_6.8_spmd.clone.sunk | while | flops 3147330 | bytes 10687221 | solution.py:80
  293.5 8.3 %collective-permute-done.3 = f32[2,32,64,128]{3,2,1,0:T(8,128)} collective-permute-done((f32[2,32,64,128]{3,2,1,0:T(8,128)}, f32[2,32,64,128]{3,2,1,0:T(8,128)}, u32[]{:S(2)}, u32[]{:S(2)}) %collective-permute-start.3) | collective-permute-done | bytes 2097184 | tf_op jit(solution)/shard_map/ppermute | solution.py:17
  304.7 38.5 %while.99 = (s32[]{:T(128)}, f32[32,8192]{1,0:T(8,128)S(1)}, f32[32,8192]{1,0:T(8,128)}, s32[4]{0:T(128)S(1)}, f32[32,8192]{1,0:T(8,128)S(1)}, /*index=5*/f32[4,...) while((s32[]{:T(128)}, f32[32,8192]{1,0:T(8,128)S(1)}, ...), condition=%wide.region_9.11_spmd.clone, body=%wide.region_8.10_spmd.clone.sunk | while | flops 3147330 | bytes 10687221 | solution.py:80
  343.3 7.4 %collective-permute-done.4 = f32[2,32,64,128]{3,2,1,0:T(8,128)} collective-permute-done((f32[2,32,64,128]{3,2,1,0:T(8,128)}, f32[2,32,64,128]{3,2,1,0:T(8,128)}, u32[]{:S(2)}, u32[]{:S(2)}) %collective-permute-start.4) | collective-permute-done | bytes 2097184 | tf_op jit(solution)/shard_map/ppermute | solution.py:17
  353.6 38.7 %while.100 = (s32[]{:T(128)}, f32[32,8192]{1,0:T(8,128)S(1)}, f32[32,8192]{1,0:T(8,128)}, s32[4]{0:T(128)S(1)}, f32[32,8192]{1,0:T(8,128)S(1)}, /*index=5*/f32[4...) while((s32[]{:T(128)}, f32[32,8192]{1,0:T(8,128)S(1)}, ...), condition=%wide.region_11.13_spmd.clone, body=%wide.region_10.12_spmd.clone.sunk | while | flops 3147330 | bytes 10687221 | solution.py:80
  413.7 8.9 %all-to-all-done.2 = f32[4,1,65536]{2,1,0:T(1,128)S(1)} async-done(((f32[4,1,65536]{2,1,0:T(1,128)}), f32[4,1,65536]{2,1,0:T(1,128)S(1)}, u32[]{:S(2)}, u32[]{:S(2)}) %all-to-all-start.2) | async-done | bytes 1048608 | tf_op jit(solution)/shard_map/all_to_all | solution.py:102
  423.6 4.5 all-to-all-start.3
  428.1 4.6 %reduce.3 = f32[4,65536]{1,0:T(4,128)S(1)} reduce(f32[4,1,65536]{2,1,0:T(1,128)} %copy-done.4, f32[]{:T(128)} %broadcast.711), dimensions={1}, to_apply=%all_to_all.54.reduce_sub_computation | reduce | bytes 2097156 | tf_op jit(solution)/shard_map/all_to_all | solution.py:102
  442.6 4.6 %reduce.4 = f32[4,65536]{1,0:T(4,128)S(1)} reduce(f32[4,1,65536]{2,1,0:T(1,128)} %all-to-all-done.3, f32[]{:T(128)} %broadcast.711), dimensions={1}, to_apply=%all_to_all.58.reduce_sub_computation | reduce | bytes 2097156 | tf_op jit(solution)/shard_map/all_to_all | solution.py:103
  455.7 5.5 %collective-permute-done.5 = f32[1,32,128]{2,1,0:T(8,128)S(1)} collective-permute-done((f32[1,32,128]{2,1,0:T(8,128)S(1)}, f32[1,32,128]{2,1,0:T(8,128)S(1)}, u32[]{:S(2)}, u32[]{:S(2)}) %collective-permute-start.5) | collective-permute-done | bytes 16416 | tf_op jit(solution)/shard_map/ppermute | solution.py:17
  (282 shorter events, 323.7 us)
Async XLA Ops:
  0.0 10.3 %copy-start = (f32[32,32,128]{2,1,0:T(8,128)S(1)}, f32[32,32,128]{2,1,0:T(8,128)}, u32[]{:S(2)}) copy-start(f32[32,32,128]{2,1,0:T(8,128)} %param.17) | copy-start | bytes 1572868
  6.1 23.0 %all-to-all-start.1 = ((f32[4,1,4096]{2,1,0:T(1,128)}), f32[4,1,4096]{2,1,0:T(1,128)S(1)}, u32[]{:S(2)}, u32[]{:S(2)}) async-start(f32[4,1,4096]{2,1,0:T(1,128)} %reshape.366), calls=%async_computation.1 | async-start | bytes 131072 | tf_op jit(solution)/shard_map/all_to_all | solution.py:47
  29.1 30.2 %all-to-all-start = ((f32[4,1,131072]{2,1,0:T(1,128)}), f32[4,1,131072]{2,1,0:T(1,128)}, u32[]{:S(2)}, u32[]{:S(2)}) async-start(f32[4,1,131072]{2,1,0:T(1,128)} %reshape.364), calls=%async_computation | async-start | bytes 4194304 | tf_op jit(solution)/shard_map/all_to_all | solution.py:47
  99.8 49.9 %collective-permute-start = (f32[2,32,64,128]{3,2,1,0:T(8,128)}, f32[2,32,64,128]{3,2,1,0:T(8,128)}, u32[]{:S(2)}, u32[]{:S(2)}) collective-permute-start(f32[2,32,64,128]{3,2,1,0:T(8,128)} %pad_maximum_fusion.1), channel_id=1, source_target_pairs={{12,0},{0,4},{4,8},{8,12},{13,1},{1,5},{5,9},{9,13},{14,2},{2,6},{... | collective-permute-start | bytes 6291464 | tf_op jit(solution)/shard_map/ppermute | solution.py:17
  101.9 1.2 copy-start.7
  152.5 48.8 %collective-permute-start.1 = (f32[2,32,64,128]{3,2,1,0:T(8,128)}, f32[2,32,64,128]{3,2,1,0:T(8,128)}, u32[]{:S(2)}, u32[]{:S(2)}) collective-permute-start(f32[2,32,64,128]{3,2,1,0:T(8,128)} %collective-permute-done), channel_id=1, source_target_pairs={{12,0},{0,4},{4,8},{8,12},{13,1},{1,5},{5,9},{9,13},{14,2},{2,6},{... | collective-permute-start | bytes 6291464 | tf_op jit(solution)/shard_map/ppermute | solution.py:17
  204.2 47.8 %collective-permute-start.2 = (f32[2,32,64,128]{3,2,1,0:T(8,128)}, f32[2,32,64,128]{3,2,1,0:T(8,128)}, u32[]{:S(2)}, u32[]{:S(2)}) collective-permute-start(f32[2,32,64,128]{3,2,1,0:T(8,128)} %collective-permute-done.1), channel_id=1, source_target_pairs={{12,0},{0,4},{4,8},{8,12},{13,1},{1,5},{5,9},{9,13},{14,2},{2,6},{... | collective-permute-start | bytes 6291464 | tf_op jit(solution)/shard_map/ppermute | solution.py:17
  254.9 46.9 %collective-permute-start.3 = (f32[2,32,64,128]{3,2,1,0:T(8,128)}, f32[2,32,64,128]{3,2,1,0:T(8,128)}, u32[]{:S(2)}, u32[]{:S(2)}) collective-permute-start(f32[2,32,64,128]{3,2,1,0:T(8,128)} %collective-permute-done.2), channel_id=1, source_target_pairs={{12,0},{0,4},{4,8},{8,12},{13,1},{1,5},{5,9},{9,13},{14,2},{2,6},{... | collective-permute-start | bytes 6291464 | tf_op jit(solution)/shard_map/ppermute | solution.py:17
  304.7 46.0 %collective-permute-start.4 = (f32[2,32,64,128]{3,2,1,0:T(8,128)}, f32[2,32,64,128]{3,2,1,0:T(8,128)}, u32[]{:S(2)}, u32[]{:S(2)}) collective-permute-start(f32[2,32,64,128]{3,2,1,0:T(8,128)} %collective-permute-done.3), channel_id=1, source_target_pairs={{12,0},{0,4},{4,8},{8,12},{13,1},{1,5},{5,9},{9,13},{14,2},{2,6},{... | collective-permute-start | bytes 6291464 | tf_op jit(solution)/shard_map/ppermute | solution.py:17
  392.4 2.5 copy-start.2
  395.1 1.3 copy-start.5
  395.1 1.3 copy-start.6
  404.7 18.0 %all-to-all-start.2 = ((f32[4,1,65536]{2,1,0:T(1,128)}), f32[4,1,65536]{2,1,0:T(1,128)S(1)}, u32[]{:S(2)}, u32[]{:S(2)}) async-start(f32[4,1,65536]{2,1,0:T(1,128)} %reshape.368), calls=%async_computation.2 | async-start | bytes 2097152 | tf_op jit(solution)/shard_map/all_to_all | solution.py:102
  422.6 1.0 copy-start.4
  423.6 19.0 %all-to-all-start.3 = ((f32[4,1,65536]{2,1,0:T(1,128)}), f32[4,1,65536]{2,1,0:T(1,128)}, u32[]{:S(2)}, u32[]{:S(2)}) async-start(f32[4,1,65536]{2,1,0:T(1,128)} %reshape.370), calls=%async_computation.3 | async-start | bytes 2097152 | tf_op jit(solution)/shard_map/all_to_all | solution.py:103
  450.9 2.6 copy-start.3
  451.0 11.1 %copy-start.1 = (f32[32,32,128]{2,1,0:T(8,128)S(1)}, f32[32,32,128]{2,1,0:T(8,128)}, u32[]{:S(2)}) copy-start(f32[32,32,128]{2,1,0:T(8,128)} %param.17) | copy-start | bytes 1572868
  455.6 5.6 %collective-permute-start.5 = (f32[1,32,128]{2,1,0:T(8,128)S(1)}, f32[1,32,128]{2,1,0:T(8,128)S(1)}, u32[]{:S(2)}, u32[]{:S(2)}) collective-permute-start(f32[1,32,128]{2,1,0:T(8,128)S(1)} %slice.124), channel_id=1, source_target_pairs={{12,0},{0,4},{4,8},{8,12},{13,1},{1,5},{5,9},{9,13},{14,2},{2,6},{... | collective-permute-start | bytes 49160 | tf_op jit(solution)/shard_map/ppermute | solution.py:17
where the time goes:
time: 472 us; the launch traced here: 462 us
  local copies, waits for them, and re-layouts  179 us (38%)
  other arithmetic  147 us (31%)
  waiting for transfers between devices  66.9 us (14%)
  matrix products  33.3 us (7%)
  starting transfers between devices  19 us (4%)
  blocking collectives  15.2 us (3%)
    add x24, other arithmetic, one_entry(): running[1] + src_real * sp_imag + src_imag * sp_real  92.9 us
    ppermute x6, waiting for transfers between devices, shifted(): return lax.ppermute(block, axis, route)  50.4 us
    gather x24, local copies, waits for them, and re-layouts, one_entry(): src_real = jnp.where(valid, jnp.take(source[0], safe, axis=0), 0.0)  44.2 us
    gather x24, local copies, waits for them, and re-layouts, one_entry(): src_imag = jnp.where(valid, jnp.take(source[1], safe, axis=0), 0.0)  44 us
    unnamed x27, local copies, waits for them, and re-layouts  22.9 us
    and x24, other arithmetic, one_entry(): src_real = jnp.where(valid, jnp.take(source[0], safe, axis=0), 0.0)  15.8 us
    select_n x24, other arithmetic, one_entry(): src_real = jnp.where(valid, jnp.take(source[0], safe, axis=0), 0.0)  15.6 us
    all_gather x1, blocking collectives, local(): lax.all_gather(forward(sparse_coef), 'blk', axis=1, tiled=True)  15.2 us
  transfers between devices with their start and end apart: 10, of which 9 were waited for; matrix products, arithmetic and copies ran while one was open for 50% of the time, Pallas kernels for 0%

commit v1 on v0

v1 whole, which is shorter than its diff:
```python
import numpy as np

import jax
import jax.numpy as jnp
from jax import lax
from jax.experimental import pallas as pl
from jax.experimental.pallas import tpu as pltpu
from jax.sharding import PartitionSpec as P

NN = (((1,), (0,)), ((), ()))
NT = (((1,), (1,)), ((), ()))


def halves(x):
    hi = x.astype(jnp.bfloat16)
    return hi, (x - hi.astype(jnp.float32)).astype(jnp.bfloat16)


def dot3(a, b, dims):
    def one(x, y):
        return lax.dot_general(x, y, dims, preferred_element_type=jnp.float32)

    return one(a[0], b[0]) + (one(a[0], b[1]) + one(a[1], b[0]))


def tables(rows, cols, devices, chunk):
    per = rows // devices
    e = np.arange(rows)
    phase = (np.outer(2 * e + 1, np.arange(rows)) % (4 * rows)) * (2 * np.pi / (4 * rows))
    both = np.stack([np.cos(phase), -np.sin(phase)], axis=1)
    by_device = both.reshape(devices, per // chunk, chunk, 2, rows)
    row_table = by_device.transpose(1, 0, 2, 3, 4).reshape(2 * rows, rows)
    sparse_rows = max(8, 2 * per)
    sparse_table = np.zeros((devices, sparse_rows, rows))
    sparse_table[:, : 2 * per] = both.reshape(devices, 2 * per, rows)
    twist_phase = np.outer(np.arange(cols), 2 * e + 1) * (2 * np.pi / (4 * rows * cols))
    twist = np.stack([np.cos(twist_phase), -np.sin(twist_phase)], axis=2)
    twist = twist.reshape(cols, devices, 2 * per).transpose(1, 0, 2)
    dft_phase = (np.outer(np.arange(cols), np.arange(cols)) % cols) * (2 * np.pi / cols)
    dft = np.concatenate([np.cos(dft_phase), -np.sin(dft_phase)], axis=1)
    out = (row_table, sparse_table.reshape(devices * sparse_rows, rows), twist, dft)
    return [np.asarray(t, np.float32) for t in out]


def kernel(
    nz, ns, chunk,
    dense, sparse, pattern, row_table, sparse_table, twist_all, dft,
    out,
    y, r, u, v, ysp, rsp, xs, twist,
    send1, recv1, send2, recv2, send3, recv3, twist_sem,
):
    devices = nz * ns
    blocks, qlocal, rows = dense.shape
    cols = qlocal * ns
    groups = cols // qlocal
    deep = blocks // groups
    per = rows // devices
    chunks = per // chunk
    total = blocks * nz
    span = chunk * 2 * deep
    sparse_rows = rsp.shape[1] // devices
    entries = sparse.shape[0]
    iz, js = lax.axis_index("blk"), lax.axis_index("sub")
    me = iz * ns + js

    get_twist = pltpu.make_async_copy(twist_all.at[me], twist, twist_sem)
    get_twist.start()

    def where(i):
        peer = lax.rem(me + i, devices)
        return peer, {"blk": peer // ns, "sub": lax.rem(peer, ns)}

    barrier = pltpu.get_barrier_semaphore()

    @pl.loop(1, devices)
    def _(i):
        pl.semaphore_signal(
            barrier, inc=1, device_id=where(i)[1], device_id_type=pl.DeviceIdType.MESH
        )

    for i in range(entries):
        wide = jnp.concatenate([sparse[i]] * groups, axis=0)
        ysp[i] = dot3(halves(sparse_table[...]), halves(wide), NT)

    pl.semaphore_wait(barrier, devices - 1)

    def at(ref, ch, dev):
        return ref.at[pl.ds(pl.multiple_of((ch * devices + dev) * span, span), span), :]

    def move(src, dst, sends, recvs, ch, i):
        peer, ident = where(i)
        return pltpu.make_async_remote_copy(
            src_ref=at(src, ch, peer), dst_ref=at(dst, ch, me),
            send_sem=sends.at[ch, i], recv_sem=recvs.at[ch, i],
            device_id=ident, device_id_type=pl.DeviceIdType.MESH,
        )

    def move_sparse(n, i):
        peer, ident = where(i)

        def part(ref, dev):
            start = pl.multiple_of(dev * sparse_rows, sparse_rows)
            return ref.at[n, pl.ds(start, sparse_rows), :]

        return pltpu.make_async_remote_copy(
            src_ref=part(ysp, peer), dst_ref=part(rsp, me),
            send_sem=send3.at[n, i], recv_sem=recv3.at[n, i],
            device_id=ident, device_id_type=pl.DeviceIdType.MESH,
        )

    for n in range(entries):
        @pl.loop(1, devices)
        def _(i):
            move_sparse(n, i).start()
        own = pl.ds(pl.multiple_of(me * sparse_rows, sparse_rows), sparse_rows)
        rsp[n, own, :] = ysp[n, own, :]

    inputs = []
    for j in range(deep):
        inputs.append(halves(jnp.concatenate([dense[g * deep + j] for g in range(groups)], axis=0)))
    slab = devices * chunk * 2
    for ch in range(chunks):
        weights = halves(row_table[ch * slab:(ch + 1) * slab, :])
        for j in range(deep):
            y[pl.ds(ch * slab * deep + j, slab, stride=deep), :] = dot3(weights, inputs[j], NT)

        @pl.loop(1, devices)
        def _(i):
            move(y, r, send1, recv1, ch, i).start()
        own = pl.ds(pl.multiple_of((ch * devices + me) * span, span), span)
        r[own, :] = y[own, :]

    get_twist.wait()
    for n in range(entries):
        @pl.loop(1, devices)
        def _(i):
            move_sparse(n, i).wait()

    group_of = lax.broadcasted_iota(jnp.int32, (deep, cols), 1) // qlocal
    sub_group = lax.broadcasted_iota(jnp.int32, (ns, cols), 1) // qlocal
    sub_row = lax.broadcasted_iota(jnp.int32, (ns, cols), 0)
    own_lane = sub_group == sub_row

    def regroup(tiles):
        result = []
        for b in range(groups):
            got = None
            for a in range(groups):
                shift = ((a - b) * qlocal) % cols
                piece = pltpu.roll(tiles[a], shift, 1) if shift else tiles[a]
                got = piece if got is None else jnp.where(group_of == a, piece, got)
            result.append(got)
        return result

    for ch in range(chunks):
        @pl.loop(1, devices)
        def _(i):
            move(y, r, send1, recv1, ch, i).wait()

        for e in range(chunk):
            k = ch * chunk + e
            base = (e * 2) * deep
            for c in range(2):
                for z in range(nz):
                    tiles = []
                    for s in range(ns):
                        start = (ch * devices + z * ns + s) * span + base + c * deep
                        tiles.append(r[start:start + deep, :])
                    for g, tile in enumerate(regroup(tiles)):
                        start = z * blocks + g * deep
                        xs[start:start + deep, c * cols:(c + 1) * cols] = tile
            spectra = []
            for z in range(nz):
                for n in range(entries):
                    pair = []
                    for c in range(2):
                        start = z * ns * sparse_rows + 2 * k + c
                        got = rsp[n, pl.ds(start, ns, stride=sparse_rows), :]
                        pair.append(jnp.sum(jnp.where(own_lane, got, 0.0), axis=0, keepdims=True))
                    spectra.append(jnp.concatenate(pair, axis=1))
            count = len(spectra)
            fill = -count % 8
            if fill:
                spectra.append(jnp.zeros((fill, 2 * cols), jnp.float32))
            spectra = jnp.concatenate(spectra, axis=0)

            cos_q = twist[:, 2 * k:2 * k + 1]
            sin_q = twist[:, 2 * k + 1:2 * k + 2]
            base_re, base_im = dft[:, :cols], dft[:, cols:]
            t_re = cos_q * base_re - sin_q * base_im
            t_im = cos_q * base_im + sin_q * base_re
            matrix = halves(
                jnp.concatenate(
                    [
                        jnp.concatenate([t_re, t_im], axis=1),
                        jnp.concatenate([-t_im, t_re], axis=1),
                    ],
                    axis=0,
                )
            )

            x = xs[...]
            before = pltpu.roll(x, 1, 0)
            parity = lax.rem(me * per + k, 2)
            sign = (1 - 2 * parity).astype(jnp.float32)
            turned = jnp.concatenate([-before[:, cols:], before[:, :cols]], axis=1)
            spectrum = dot3(halves(x + sign * turned), matrix, NN)
            sparse_spectrum = dot3(halves(spectra), matrix, NN)
            sum_re = jnp.zeros((total, cols), jnp.float32)
            sum_im = jnp.zeros((total, cols), jnp.float32)
            for n in range(count):
                shift = lax.rem(pattern[n], total)
                a = pltpu.roll(spectrum, shift, 0)
                s_re = sparse_spectrum[n:n + 1, :cols]
                s_im = sparse_spectrum[n:n + 1, cols:]
                sum_re += a[:, :cols] * s_re - a[:, cols:] * s_im
                sum_im += a[:, :cols] * s_im + a[:, cols:] * s_re
            back = dot3(halves(jnp.concatenate([sum_re, sum_im], axis=1)), matrix, NT)
            for c in range(2):
                for z in range(nz):
                    tiles = []
                    for g in range(groups):
                        start = z * blocks + g * deep
                        tiles.append(back[start:start + deep, c * cols:(c + 1) * cols])
                    for s, tile in enumerate(regroup(tiles)):
                        start = (ch * devices + z * ns + s) * span + base + c * deep
                        u[start:start + deep, :] = tile

        @pl.loop(1, devices)
        def _(i):
            move(u, v, send2, recv2, ch, i).start()
        own = pl.ds(pl.multiple_of((ch * devices + me) * span, span), span)
        v[own, :] = u[own, :]

    for ch in range(chunks):
        @pl.loop(1, devices)
        def _(i):
            move(u, v, send2, recv2, ch, i).wait()

    weights = halves(row_table[...])
    for j in range(deep):
        got = v[pl.ds(j, 2 * rows, stride=deep), :].T
        values = dot3(halves(got), weights, NN) * (1.0 / (rows * cols))
        for g in range(groups):
            out[g * deep + j] = values[g * qlocal:(g + 1) * qlocal, :]


def solution(mesh):
    nz, ns = mesh.shape["blk"], mesh.shape["sub"]
    devices = nz * ns

    def local(dense, sparse, pattern):
        blocks, qlocal, rows = dense.shape
        cols = qlocal * ns
        per = rows // devices
        chunk = min(per, 2)
        chunks = per // chunk
        entries = sparse.shape[0]
        row_table, sparse_table, twist, dft = tables(rows, cols, devices, chunk)
        depth = 2 * rows * blocks * qlocal // cols
        f32 = jnp.float32
        vmem = pl.BlockSpec(memory_space=pltpu.VMEM)
        sparse_shape = (entries, sparse_table.shape[0], cols)

        def body(*refs):
            kernel(nz, ns, chunk, *refs)

        return pl.pallas_call(
            body,
            out_shape=jax.ShapeDtypeStruct(dense.shape, f32),
            in_specs=[
                vmem, vmem, pl.BlockSpec(memory_space=pltpu.SMEM),
                vmem, vmem, pl.BlockSpec(memory_space=pl.ANY), vmem,
            ],
            out_specs=vmem,
            scratch_shapes=[
                pltpu.VMEM((depth, cols), f32),
                pltpu.VMEM((depth, cols), f32),
                pltpu.VMEM((depth, cols), f32),
                pltpu.VMEM((depth, cols), f32),
                pltpu.VMEM(sparse_shape, f32),
                pltpu.VMEM(sparse_shape, f32),
                pltpu.VMEM((blocks * nz, 2 * cols), f32),
                pltpu.VMEM(twist.shape[1:], f32),
                pltpu.SemaphoreType.DMA((chunks, devices)),
                pltpu.SemaphoreType.DMA((chunks, devices)),
                pltpu.SemaphoreType.DMA((chunks, devices)),
                pltpu.SemaphoreType.DMA((chunks, devices)),
                pltpu.SemaphoreType.DMA((entries, devices)),
                pltpu.SemaphoreType.DMA((entries, devices)),
                pltpu.SemaphoreType.DMA,
            ],
            compiler_params=pltpu.CompilerParams(
                collective_id=0, has_side_effects=True, vmem_limit_bytes=48 * 1024 * 1024
            ),
            cost_estimate=pl.CostEstimate(
                flops=1500000000, bytes_accessed=4000000, transcendentals=0
            ),
            name="series",
        )(dense, sparse, pattern, row_table, sparse_table, twist, dft)

    return jax.shard_map(
        local,
        mesh=mesh,
        in_specs=(
            P(("groups", "blk"), "sub", None),
            P(("groups", "blk"), "sub", None),
            P("groups"),
        ),
        out_specs=P(("groups", "blk"), "sub", None),
        check_vma=False,
    )
```

time: 472 us -> 64.8 us (0.14); the launches traced: 462 us -> 64.5 us
  local copies, waits for them, and re-layouts: 179 us -> 7.14 us
  other arithmetic: 147 us -> 0 us
  waiting for transfers between devices: 66.9 us -> 0 us
  Pallas kernels: 0 us -> 57.4 us
  matrix products: 33.3 us -> 0 us
  starting transfers between devices: 19 us -> 0 us
  blocking collectives: 15.2 us -> 0 us
    add x27 -> x0, other arithmetic: 93.7 us -> none  [the longest x24 92.9 us: one_entry(): running[1] + src_real * sp_imag + src_imag * sp_real]
    gather x48 -> x0, local copies, waits for them, and re-layouts: 88.2 us -> none  [the longest x24 44.2 us: one_entry(): src_real = jnp.where(valid, jnp.take(source[0], safe, axis=0), 0.0)]
    pallas_call x0 -> x1, Pallas kernels: none -> 57.4 us  [local(): pl.pallas_call(body, out_shape=jax.ShapeDtypeStruct(dense.shape, f32), in...]
    ppermute x6 -> x0, waiting for transfers between devices: 50.4 us -> none  [shifted(): return lax.ppermute(block, axis, route)]
    dot_general x18 -> x0, matrix products: 33.3 us -> none  [the longest x2 4.15 us: forward(): jnp.einsum('rxs,xl->rsl', partial_real, outer_sine, precision=exact_setting)]
    all_to_all x7 -> x0, local copies, waits for them, and re-layouts: 19.5 us -> none  [the longest x3 8.75 us: forward(): lax.all_to_all(stacked, 'sub', split_axis=3, concat_axis=2, tiled=True)]
    all_to_all x4 -> x0, other arithmetic: 17.9 us -> none  [the longest x2 8.59 us: forward(): lax.all_to_all(stacked, 'sub', split_axis=3, concat_axis=2, tiled=True)]
    all_to_all x4 -> x0, starting transfers between devices: 16.6 us -> none  [the longest x2 8.66 us: forward(): lax.all_to_all(stacked, 'sub', split_axis=3, concat_axis=2, tiled=True)]
  transfers between devices with their start and end apart: 10 -> 0, of which waited for: 9 -> 0; matrix products, arithmetic and copies ran while one was open for 50% -> 0% of each run, Pallas kernels for 0% -> 0%
where the time goes in v1:
time: 64.8 us; the launch traced here: 64.5 us
  Pallas kernels  57.4 us (89%)
  local copies, waits for them, and re-layouts  7.14 us (11%)
    pallas_call x1, Pallas kernels, local(): pl.pallas_call(body, out_shape=jax.ShapeDtypeStruct(dense.shape, f32), in...  57.4 us
    unnamed x15, local copies, waits for them, and re-layouts  7.14 us

profile of v1, /device:TPU:0, one launch (start us, length us, event | category | flops | bytes accessed | tf_op | source)
XLA Modules:
  0.0 64.5 jit_solution(4080000345781000217)
XLA Ops:
  0.0 0.0 copy-start
  0.0 1.0 %copy-done = f32[32,32,128]{2,1,0:T(8,128)S(1)} copy-done((f32[32,32,128]{2,1,0:T(8,128)S(1)}, f32[32,32,128]{2,1,0:T(8,128)}, u32[]{:S(2)}) %copy-start) | copy-done | bytes 524312
  1.0 0.0 copy-start.1
  1.0 0.7 %copy-done.1 = f32[1,32,128]{2,1,0:T(8,128)S(1)} copy-done((f32[1,32,128]{2,1,0:T(8,128)S(1)}, f32[1,32,128]{2,1,0:T(8,128)}, u32[]{:S(2)}) %copy-start.1) | copy-done | bytes 16408
  1.8 0.0 copy-start.2
  1.8 0.7 %copy-done.2 = s32[4]{0:T(128)S(1)} copy-done((s32[4]{0:T(128)S(1)}, s32[4]{0:T(128)}, u32[]{:S(2)}) %copy-start.2) | copy-done | bytes 40
  2.4 0.0 copy-start.3
  2.4 1.2 %copy-done.3 = f32[16,128,16]{2,1,0:T(8,128)S(1)} copy-done((f32[16,128,16]{2,1,0:T(8,128)S(1)}, f32[16,128,16]{2,1,0:T(8,128)}, u32[]{:S(2)}) %copy-start.3) | copy-done | bytes 131096
  3.6 0.0 copy-start.4
  3.6 0.9 %copy-done.4 = f32[128,256]{1,0:T(8,128)S(1)} copy-done((f32[128,256]{1,0:T(8,128)S(1)}, f32[128,256]{1,0:T(8,128)}, u32[]{:S(2)}) %copy-start.4) | copy-done | bytes 131096
  4.5 0.0 copy-start.5
  4.5 0.9 %copy-done.5 = f32[256,128]{1,0:T(8,128)S(1)} copy-done((f32[256,128]{1,0:T(8,128)S(1)}, f32[256,128]{1,0:T(8,128)}, u32[]{:S(2)}) %copy-start.5) | copy-done | bytes 131096
  5.5 0.0 copy-start.6
  5.5 0.9 %copy-done.6 = f32[256,128]{1,0:T(8,128)S(1)} copy-done((f32[256,128]{1,0:T(8,128)S(1)}, f32[256,128]{1,0:T(8,128)}, u32[]{:S(2)}) %copy-start.6) | copy-done | bytes 131096
  6.4 57.4 %series.1 = f32[32,32,128]{2,1,0:T(8,128)S(1)} custom-call(f32[32,32,128]{2,1,0:T(8,128)S(1)} %copy-done, f32[1,32,128]{2,1,0:T(8,128)S(1)} %copy-done.1, s32[4]{0:T(128)S(1)} %copy-done.2, f32[256,128]{1,0:T(8,128)S(1)} %copy-done.6, f32[256,128]{1,0:T(8,128)S(1)} %copy-done.5, f32[16,128,16]{2,1,0:T(8,128)S(1)} %copy-done.3, f32[128,256]{1,0:T(8,128)S(1)} %copy-done.4), custom_call_target="tpu_custom_call" | custom-call | flops 1500000000 | bytes 4000000 | tf_op jit(solution)/shard_map/series/pallas_call | solution.py:268
  63.7 0.8 %copy.9 = f32[32,32,128]{2,1,0:T(8,128)} copy(f32[32,32,128]{2,1,0:T(8,128)S(1)} %series.1) | data formatting | bytes 1048576
Async XLA Ops:
  0.0 1.0 %copy-start = (f32[32,32,128]{2,1,0:T(8,128)S(1)}, f32[32,32,128]{2,1,0:T(8,128)}, u32[]{:S(2)}) copy-start(f32[32,32,128]{2,1,0:T(8,128)} %refs_0_.1) | copy-start | bytes 1572868
  1.0 0.7 %copy-start.1 = (f32[1,32,128]{2,1,0:T(8,128)S(1)}, f32[1,32,128]{2,1,0:T(8,128)}, u32[]{:S(2)}) copy-start(f32[1,32,128]{2,1,0:T(8,128)} %refs_1_.1) | copy-start | bytes 49156
  1.8 0.7 %copy-start.2 = (s32[4]{0:T(128)S(1)}, s32[4]{0:T(128)}, u32[]{:S(2)}) copy-start(s32[4]{0:T(128)} %refs_2_.1) | copy-start | bytes 52
  2.4 1.2 %copy-start.3 = (f32[16,128,16]{2,1,0:T(8,128)S(1)}, f32[16,128,16]{2,1,0:T(8,128)}, u32[]{:S(2)}) copy-start(f32[16,128,16]{2,1,0:T(8,128)} %constant.10.clone.refs_5_) | copy-start | bytes 393220
  3.6 0.9 %copy-start.4 = (f32[128,256]{1,0:T(8,128)S(1)}, f32[128,256]{1,0:T(8,128)}, u32[]{:S(2)}) copy-start(f32[128,256]{1,0:T(8,128)} %constant.11.clone.refs_6_) | copy-start | bytes 393220
  4.5 0.9 %copy-start.5 = (f32[256,128]{1,0:T(8,128)S(1)}, f32[256,128]{1,0:T(8,128)}, u32[]{:S(2)}) copy-start(f32[256,128]{1,0:T(8,128)} %constant.9.clone.refs_4_) | copy-start | bytes 393220
  5.5 0.9 %copy-start.6 = (f32[256,128]{1,0:T(8,128)S(1)}, f32[256,128]{1,0:T(8,128)}, u32[]{:S(2)}) copy-start(f32[256,128]{1,0:T(8,128)} %constant.8.clone.refs_3_) | copy-start | bytes 393220

commit v2 on v1

--- a/solution.py
+++ b/solution.py
@@ -44,10 +44,11 @@
 
 def kernel(
     nz, ns, chunk,
-    dense, sparse, pattern, row_table, sparse_table, twist_all, dft,
+    dense_far, sparse_far, pattern, row_far, sparse_table_far, twist_far, dft_far,
     out,
     y, r, u, v, ysp, rsp, xs, twist,
-    send1, recv1, send2, recv2, send3, recv3, twist_sem,
+    send1, recv1, send2, recv2, send3, recv3,
+    dense, sparse, row_table, sparse_table, dft, load_sem,
 ):
     devices = nz * ns
     blocks, qlocal, rows = dense.shape
@@ -63,8 +64,17 @@
     iz, js = lax.axis_index("blk"), lax.axis_index("sub")
     me = iz * ns + js
 
-    get_twist = pltpu.make_async_copy(twist_all.at[me], twist, twist_sem)
-    get_twist.start()
+    loads = [
+        pltpu.make_async_copy(far, near, load_sem.at[n])
+        for n, (far, near) in enumerate(
+            [
+                (sparse_table_far, sparse_table), (sparse_far, sparse), (row_far, row_table),
+                (dense_far, dense), (twist_far.at[me], twist), (dft_far, dft),
+            ]
+        )
+    ]
+    for load in loads:
+        load.start()
 
     def where(i):
         peer = lax.rem(me + i, devices)
@@ -78,6 +88,8 @@
             barrier, inc=1, device_id=where(i)[1], device_id_type=pl.DeviceIdType.MESH
         )
 
+    loads[0].wait()
+    loads[1].wait()
     for i in range(entries):
         wide = jnp.concatenate([sparse[i]] * groups, axis=0)
         ysp[i] = dot3(halves(sparse_table[...]), halves(wide), NT)
@@ -115,6 +127,8 @@
         own = pl.ds(pl.multiple_of(me * sparse_rows, sparse_rows), sparse_rows)
         rsp[n, own, :] = ysp[n, own, :]
 
+    loads[2].wait()
+    loads[3].wait()
     inputs = []
     for j in range(deep):
         inputs.append(halves(jnp.concatenate([dense[g * deep + j] for g in range(groups)], axis=0)))
@@ -130,7 +144,8 @@
         own = pl.ds(pl.multiple_of((ch * devices + me) * span, span), span)
         r[own, :] = y[own, :]
 
-    get_twist.wait()
+    loads[4].wait()
+    loads[5].wait()
     for n in range(entries):
         @pl.loop(1, devices)
         def _(i):
@@ -260,6 +275,7 @@
         depth = 2 * rows * blocks * qlocal // cols
         f32 = jnp.float32
         vmem = pl.BlockSpec(memory_space=pltpu.VMEM)
+        far = pl.BlockSpec(memory_space=pltpu.HBM)
         sparse_shape = (entries, sparse_table.shape[0], cols)
 
         def body(*refs):
@@ -269,8 +285,8 @@
             body,
             out_shape=jax.ShapeDtypeStruct(dense.shape, f32),
             in_specs=[
-                vmem, vmem, pl.BlockSpec(memory_space=pltpu.SMEM),
-                vmem, vmem, pl.BlockSpec(memory_space=pl.ANY), vmem,
+                far, far, pl.BlockSpec(memory_space=pltpu.SMEM),
+                far, far, far, far,
             ],
             out_specs=vmem,
             scratch_shapes=[
@@ -288,10 +304,15 @@
                 pltpu.SemaphoreType.DMA((chunks, devices)),
                 pltpu.SemaphoreType.DMA((entries, devices)),
                 pltpu.SemaphoreType.DMA((entries, devices)),
-                pltpu.SemaphoreType.DMA,
+                pltpu.VMEM(dense.shape, f32),
+                pltpu.VMEM(sparse.shape, f32),
+                pltpu.VMEM(row_table.shape, f32),
+                pltpu.VMEM(sparse_table.shape, f32),
+                pltpu.VMEM(dft.shape, f32),
+                pltpu.SemaphoreType.DMA((6,)),
             ],
             compiler_params=pltpu.CompilerParams(
-                collective_id=0, has_side_effects=True, vmem_limit_bytes=48 * 1024 * 1024
+                collective_id=0, has_side_effects=True, vmem_limit_bytes=64 * 1024 * 1024
             ),
             cost_estimate=pl.CostEstimate(
                 flops=1500000000, bytes_accessed=4000000, transcendentals=0

time: 64.8 us -> 60.2 us (0.929)
  local copies, waits for them, and re-layouts: 7.14 us -> 1.87 us
  Pallas kernels: 57.4 us -> 58.2 us
    unnamed x15 -> x1, local copies, waits for them, and re-layouts: 7.14 us -> 1.87 us
    pallas_call x1, Pallas kernels: 57.4 us -> 58.2 us  [local(): pl.pallas_call(body, out_shape=jax.ShapeDtypeStruct(dense.shape, f32), in...]
where the time goes in v2:
time: 60.2 us; the launch traced here: 60 us
  Pallas kernels  58.2 us (97%)
  local copies, waits for them, and re-layouts  1.87 us (3%)
    pallas_call x1, Pallas kernels, local(): pl.pallas_call(body, out_shape=jax.ShapeDtypeStruct(dense.shape, f32), in...  58.2 us
    unnamed x1, local copies, waits for them, and re-layouts  1.87 us

profile of v2, /device:TPU:0, one launch (start us, length us, event | category | flops | bytes accessed | tf_op | source)
XLA Modules:
  0.0 60.0 jit_solution(9242151901504758614)
XLA Ops:
  0.0 58.2 %series.1 = f32[32,32,128]{2,1,0:T(8,128)} custom-call(f32[32,32,128]{2,1,0:T(8,128)} %refs_0_.1, f32[1,32,128]{2,1,0:T(8,128)} %refs_1_.1, s32[4]{0:T(128)} %refs_2_.1, f32[256,128]{1,0:T(8,128)} %constant.8.clone.refs_3_, f32[256,128]{1,0:T(8,128)} %constant.9.clone.refs_4_, f32[16,128,16]{2,1,0:T(8,128)} %constant.10.clone.refs_5_, ...), custom_call_target="tpu_custom_call" | custom-call | flops 1500000000 | bytes 4000000 | tf_op jit(solution)/shard_map/series/pallas_call | solution.py:284
  58.2 1.9 %copy.9 = f32[32,32,128]{2,1,0:T(8,128)} copy(f32[32,32,128]{2,1,0:T(8,128)} %series.1) | data formatting | bytes 1048576
